TPU v7x, 128 devices: a whole 4x4x4 slice. The times are simulated.
128 devices in a mesh: row: 8 (over y_lo, z), col: 16 (over y_hi, x, core).
Axes of the slice: x: 4, y: 4 (y_hi: 2, y_lo: 2; y = y_hi * 2 + y_lo), z: 4, core: 2. Of those that a mesh axis runs over, the one named last changes fastest.
Arguments:
- eigvecs: float32 [65536, 4096], P(('row', 'col')), may hold values from -6 to 6
- panels: float32 [3, 256, 65536], P(None, None, ('row', 'col')), may hold values from -0.09375 to 0.09375
- tri_factors: float32 [3, 256, 256], replicated, may hold values from -0.2 to 0.6, as said below
Outputs:
- back: float32 [65536, 4096], P('row', 'col')
Inputs may be any that keep to these rules, and one draw needn't show every extreme that they name: `tri_factors`: each factor is upper triangular; diagonal entries lie in 0.2 to 0.6.
All inputs are finite; a program needn't handle non-finite values.
Results may differ from a plain program's by a relative error of at most 0.00013.
Values sent between devices are 32-bit elements; how exact they have to be, the bound alone decides.
No kernel may reach another device: no remote copies, remote signals or barrier semaphores. Data moves between devices by JAX's collectives and lax.ppermute only.
A program may use at most 128 MiB of HBM per device.

v0:
```python
import jax
import jax.numpy as jnp
from jax import lax
from jax.sharding import PartitionSpec as P


def product(left, right):
    return jnp.dot(left, right, precision=lax.Precision.HIGHEST, preferred_element_type=jnp.float32)


def spread(panel_t, right):
    return lax.dot_general(
        panel_t,
        right,
        (((0,), (0,)), ((), ())),
        precision=lax.Precision.HIGHEST,
        preferred_element_type=jnp.float32,
    )


def shaped(raw, start, offset):
    count = raw.shape[0]
    width = raw.shape[1]
    place = start + lax.broadcasted_iota(jnp.int32, (count, width), 1)
    limit = offset + lax.broadcasted_iota(jnp.int32, (count, width), 0)
    return jnp.where(
        place < limit, jnp.float32(0.0), jnp.where(place == limit, jnp.float32(1.0), raw)
    )


def apply_chain(block, vectors, tri_factors, total_single):
    for index in reversed(range(len(vectors))):
        w_block = total_single(product(vectors[index], block))
        block = block - spread(vectors[index], product(tri_factors[index], w_block))
    return block


def tile_single(values):
    return lax.psum(values, "row")


def on_device(eigvecs, panels, tri_factors):
    block_size = tri_factors.shape[1]
    count = tri_factors.shape[0]
    tiles = lax.all_to_all(eigvecs, "col", split_axis=1, concat_axis=0, tiled=True)
    gathered = lax.all_gather(panels, "col", axis=2, tiled=True)
    start = lax.axis_index("row") * tiles.shape[0]
    vectors = [shaped(gathered[index], start, (index + 1) * block_size) for index in range(count)]
    return apply_chain(tiles, vectors, tri_factors, tile_single)


def solution(mesh):
    in_specs = (P(("row", "col"), None), P(None, None, ("row", "col")), P())
    out_specs = P("row", "col")
    return jax.shard_map(
        on_device, mesh=mesh, in_specs=in_specs, out_specs=out_specs, check_vma=False
    )
```

profile of v0, /device:TPU:0, one launch (start us, length us, event | category | flops | bytes accessed | tf_op | source)
XLA Modules:
  0.0 585.3 jit_solution(4360634410430133219)
XLA Ops:
  6.5 0.0 all-gather.2.cloned.1.call-start
  6.5 0.7 all-gather.2.cloned.1.call-update
  7.3 7.7 %copy.7 = f32[64,16,8,256]{3,2,0,1:T(8,128)} copy(f32[64,16,8,256]{3,2,1,0:T(8,128)} %bitcast.50) | data formatting | bytes 16777216 | tf_op jit(solution)/shard_map/all_to_all | solution.py:45
  14.9 7.2 %all-to-all-start = ((f32[512,16,256]{2,0,1:T(8,128)}), f32[512,16,256]{2,0,1:T(8,128)}, u32[]{:S(2)}, u32[]{:S(2)}) async-start(f32[512,16,256]{2,0,1:T(8,128)} %bitcast.49), calls=%async_computation | async-start | bytes 16777216 | tf_op jit(solution)/shard_map/all_to_all | solution.py:45
  22.1 0.0 all-reduce.4.cloned.1.call-start
  22.2 127.0 %all-to-all-done = f32[512,16,256]{2,0,1:T(8,128)} async-done(((f32[512,16,256]{2,0,1:T(8,128)}), f32[512,16,256]{2,0,1:T(8,128)}, u32[]{:S(2)}, u32[]{:S(2)}) %all-to-all-start) | async-done | bytes 8388640 | tf_op jit(solution)/shard_map/all_to_all | solution.py:45
  149.2 104.7 %all-gather.2.cloned.1.call-done = f32[3,256,8192]{2,1,0:T(8,128)} async-done(((f32[3,256,512]{2,1,0:T(8,128)}), f32[3,256,8192]{2,1,0:T(8,128)}) %all-gather.2.cloned.1.call-update) | async-done | bytes 25165840 | tf_op jit(solution)/shard_map/all_gather | solution.py:46
  253.9 0.0 copy-start.2
  253.9 14.9 %fusion.4 = f32[256,256]{1,0:T(8,128)} fusion(f32[8192,256]{1,0:T(8,128)} %bitcast.1, f32[3,256,8192]{2,1,0:T(8,128)} %all-gather.2.cloned.1.call-done, s32[8192]{0:T(1024)S(1)} %iota_add_fusion, s32[256]{0:T(256)S(1)} %iota_add_fusion.3), kind=kOutput, calls=%fused_computation.10 | convolution fusion | flops 6450839552 | bytes 17073152 | tf_op jit(solution)/shard_map/dot_general | solution.py:8
  268.8 0.0 all-reduce.4.cloned.1.call-update
  268.8 0.0 all-reduce.6.cloned.1.call-start
  268.9 72.0 %all-reduce.4.cloned.1.call-done = f32[256,256]{1,0:T(8,128)} async-done(((f32[256,256]{1,0:T(8,128)}), f32[256,256]{1,0:T(8,128)}) %all-reduce.4.cloned.1.call-update) | async-done | bytes 262160 | tf_op jit(solution)/shard_map/psum | solution.py:39
  340.8 0.0 copy-done.2
  340.8 1.5 fusion.50
  342.4 17.6 %convolution_subtract_fusion.2 = f32[8192,256]{1,0:T(8,128)S(1)} fusion(f32[8192,256]{1,0:T(8,128)} %bitcast.1, f32[256,256]{1,0:T(8,128)S(1)} %fusion.50, f32[3,256,8192]{2,1,0:T(8,128)} %all-gather.2.cloned.1.call-done, s32[8192]{0:T(1024)S(1)} %iota_add_fusion, s32[256]{0:T(256)S(1)} %iota_add_fusion.3), kind=kOutput, calls=%fused_computation.2 | convolution fusion | flops 6452936704 | bytes 25461760 | tf_op jit(solution)/shard_map/dot_general | solution.py:12
  360.0 0.0 copy-start
  360.1 3.4 copy-done
  363.4 12.3 %fusion.17 = f32[256,256]{1,0:T(8,128)} fusion(f32[8192,256]{1,0:T(8,128)S(1)} %convolution_subtract_fusion.2, f32[3,256,8192]{2,1,0:T(8,128)} %all-gather.2.cloned.1.call-done, s32[8192]{0:T(1024)S(1)} %iota_add_fusion, s32[256]{0:T(256)S(1)} %iota_add_fusion.2), kind=kOutput, calls=%fused_computation.22 | convolution fusion | flops 6450839552 | bytes 17073152 | tf_op jit(solution)/shard_map/dot_general | solution.py:8
  375.8 0.0 all-reduce.6.cloned.1.call-update
  375.8 0.2 all-reduce.8.cloned.1.call-start
  376.0 73.5 %all-reduce.6.cloned.1.call-done = f32[256,256]{1,0:T(8,128)} async-done(((f32[256,256]{1,0:T(8,128)}), f32[256,256]{1,0:T(8,128)}) %all-reduce.6.cloned.1.call-update) | async-done | bytes 262160 | tf_op jit(solution)/shard_map/psum | solution.py:39
  449.5 1.5 fusion.48
  451.0 17.2 %convolution_subtract_fusion.1 = f32[8192,256]{1,0:T(8,128)S(1)} fusion(f32[8192,256]{1,0:T(8,128)} %copy-done, f32[256,256]{1,0:T(8,128)S(1)} %fusion.48, f32[3,256,8192]{2,1,0:T(8,128)} %all-gather.2.cloned.1.call-done, s32[8192]{0:T(1024)S(1)} %iota_add_fusion, s32[256]{0:T(256)S(1)} %iota_add_fusion.2), kind=kOutput, calls=%fused_computation.1 | convolution fusion | flops 6452936704 | bytes 25461760 | tf_op jit(solution)/shard_map/dot_general | solution.py:12
  468.2 0.0 copy-start.1
  468.2 3.4 copy-done.1
  471.6 12.5 %fusion.20 = f32[256,256]{1,0:T(8,128)} fusion(f32[8192,256]{1,0:T(8,128)S(1)} %convolution_subtract_fusion.1, f32[3,256,8192]{2,1,0:T(8,128)} %all-gather.2.cloned.1.call-done, s32[8192]{0:T(1024)S(1)} %iota_add_fusion, s32[256]{0:T(256)S(1)} %iota_add_fusion.1), kind=kOutput, calls=%fused_computation.23 | convolution fusion | flops 6450839552 | bytes 17073152 | tf_op jit(solution)/shard_map/dot_general | solution.py:8
  484.1 0.0 all-reduce.8.cloned.1.call-update
  484.1 73.7 %all-reduce.8.cloned.1.call-done = f32[256,256]{1,0:T(8,128)} async-done(((f32[256,256]{1,0:T(8,128)}), f32[256,256]{1,0:T(8,128)}) %all-reduce.8.cloned.1.call-update) | async-done | bytes 262160 | tf_op jit(solution)/shard_map/psum | solution.py:39
  557.8 1.5 fusion.46
  559.4 19.2 %convolution_subtract_fusion = f32[8192,256]{1,0:T(8,128)} fusion(f32[8192,256]{1,0:T(8,128)} %copy-done.1, f32[256,256]{1,0:T(8,128)S(1)} %fusion.46, f32[3,256,8192]{2,1,0:T(8,128)} %all-gather.2.cloned.1.call-done, s32[8192]{0:T(1024)S(1)} %iota_add_fusion, s32[256]{0:T(256)S(1)} %iota_add_fusion.1), kind=kOutput, calls=%fused_computation | convolution fusion | flops 6452936704 | bytes 25461760 | tf_op jit(solution)/shard_map/dot_general | solution.py:12
  (4 shorter events, 0.0 us)
Async XLA Ops:
  6.5 247.3 %all-gather.2.cloned.1.call-start = ((), (), s32[]{:S(2)}) async-start(), calls=%async_computation.1 | async-start | bytes 26738688 | tf_op jit(solution)/shard_map/all_gather | solution.py:46
  14.9 134.3 %all-to-all-start = ((f32[512,16,256]{2,0,1:T(8,128)}), f32[512,16,256]{2,0,1:T(8,128)}, u32[]{:S(2)}, u32[]{:S(2)}) async-start(f32[512,16,256]{2,0,1:T(8,128)} %bitcast.49), calls=%async_computation | async-start | bytes 16777216 | tf_op jit(solution)/shard_map/all_to_all | solution.py:45
  22.1 318.7 %all-reduce.4.cloned.1.call-start = ((), (), s32[]{:S(2)}) async-start(), calls=%async_computation.2 | async-start | bytes 524288 | tf_op jit(solution)/shard_map/psum | solution.py:39
  253.9 87.0 %copy-start.2 = (f32[3,256,256]{2,1,0:T(8,128)S(1)}, f32[3,256,256]{2,1,0:T(8,128)}, u32[]{:S(2)}) copy-start(f32[3,256,256]{2,1,0:T(8,128)} %param.5) | copy-start | bytes 2359300
  268.8 180.7 %all-reduce.6.cloned.1.call-start = ((), (), s32[]{:S(2)}) async-start(), calls=%async_computation.3 | async-start | bytes 524288 | tf_op jit(solution)/shard_map/psum | solution.py:39
  360.0 3.4 copy-start
  375.8 182.1 %all-reduce.8.cloned.1.call-start = ((), (), s32[]{:S(2)}) async-start(), calls=%async_computation.4 | async-start | bytes 524288 | tf_op jit(solution)/shard_map/psum | solution.py:39
  468.2 3.4 copy-start.1
Sparse Core Ops, SparseCore 0:
  9.8 243.9 all-gather.1
  268.9 71.8 all-reduce.3
  375.9 73.5 all-reduce.5
  484.3 73.5 all-reduce.7
where the time goes:
time: 591 us; the launch traced here: 585 us
  waiting for transfers between devices  452 us (76%)
  matrix products  98.3 us (17%)
  local copies, waits for them, and re-layouts  14.5 us (2%)
  between operations  13.5 us (2%)
  starting transfers between devices  7.47 us (1%)
    psum x3, waiting for transfers between devices, tile_single(): return lax.psum(values, 'row')  219 us
    all_to_all x1, waiting for transfers between devices, on_device(): lax.all_to_all(eigvecs, 'col', split_axis=1, concat_axis=0, tiled=True)  127 us
    all_gather x1, waiting for transfers between devices, on_device(): gathered = lax.all_gather(panels, 'col', axis=2, tiled=True)  105 us
    dot_general x3, matrix products, spread(): lax.dot_general(panel_t, right, (((0,), (0,)), ((), ())), precision=lax.P...  54 us
    dot_general x6, matrix products, product(): jnp.dot(left, right, precision=lax.Precision.HIGHEST, preferred_element_t...  44.3 us
  transfers between devices with their start and end apart: 5, of which 5 were waited for; matrix products, arithmetic and copies ran while one was open for 1% of the time, Pallas kernels for 0%

commit v1 on v0

--- a/solution.py
+++ b/solution.py
@@ -42,7 +42,10 @@
 def on_device(eigvecs, panels, tri_factors):
     block_size = tri_factors.shape[1]
     count = tri_factors.shape[0]
-    tiles = lax.all_to_all(eigvecs, "col", split_axis=1, concat_axis=0, tiled=True)
+    tiles = jnp.concatenate(
+        lax.all_to_all(jnp.stack(jnp.split(eigvecs, lax.axis_size("col"), axis=1)), "col", 0, 0),
+        axis=0,
+    )
     gathered = lax.all_gather(panels, "col", axis=2, tiled=True)
     start = lax.axis_index("row") * tiles.shape[0]
     vectors = [shaped(gathered[index], start, (index + 1) * block_size) for index in range(count)]

time: 591 us -> 572 us (0.968)
  waiting for transfers between devices: 452 us -> 409 us
  local copies, waits for them, and re-layouts: 14.5 us -> 36.8 us
    all_gather x1, waiting for transfers between devices: 105 us -> 51.4 us  [on_device(): gathered = lax.all_gather(panels, 'col', axis=2, tiled=True)]
    unnamed x6 -> x21, local copies, waits for them, and re-layouts: 6.79 us -> 34.9 us
    all_to_all x1, waiting for transfers between devices: 127 us -> 138 us  [on_device(): lax.all_to_all(jnp.stack(jnp.split(eigvecs, lax.axis_size('col'), axis=1)...]
    all_to_all x1 -> x0, local copies, waits for them, and re-layouts: 7.69 us -> none  [on_device(): lax.all_to_all(eigvecs, 'col', split_axis=1, concat_axis=0, tiled=True)]
  transfers between devices with their start and end apart: 5 -> 5, of which waited for: 5 -> 5; matrix products, arithmetic and copies ran while one was open for 1% -> 5% of each run, Pallas kernels for 0% -> 0%
where the time goes in v1:
time: 572 us; the launch traced here: 565 us
  waiting for transfers between devices  409 us (72%)
  matrix products  98.3 us (17%)
  local copies, waits for them, and re-layouts  36.8 us (6%)
  between operations  13.5 us (2%)
  starting transfers between devices  7.6 us (1%)
    psum x3, waiting for transfers between devices, tile_single(): return lax.psum(values, 'row')  219 us
    all_to_all x1, waiting for transfers between devices, on_device(): lax.all_to_all(jnp.stack(jnp.split(eigvecs, lax.axis_size('col'), axis=1)...  138 us
    dot_general x3, matrix products, spread(): lax.dot_general(panel_t, right, (((0,), (0,)), ((), ())), precision=lax.P...  54 us
    all_gather x1, waiting for transfers between devices, on_device(): gathered = lax.all_gather(panels, 'col', axis=2, tiled=True)  51.4 us
    dot_general x6, matrix products, product(): jnp.dot(left, right, precision=lax.Precision.HIGHEST, preferred_element_t...  44.3 us
    unnamed x21, local copies, waits for them, and re-layouts  34.9 us
  transfers between devices with their start and end apart: 5, of which 5 were waited for; matrix products, arithmetic and copies ran while one was open for 5% of the time, Pallas kernels for 0%

profile of v1, /device:TPU:0, one launch (start us, length us, event | category | flops | bytes accessed | tf_op | source)
XLA Modules:
  0.0 565.3 jit_solution(2423590264848819441)
XLA Ops:
  6.5 0.0 all-gather.2.cloned.1.call-start
  6.5 0.7 all-gather.2.cloned.1.call-update
  7.3 1.9 bitcast_dynamic-update-slice_fusion.15
  9.1 1.9 bitcast_dynamic-update-slice_fusion.14
  11.0 1.9 bitcast_dynamic-update-slice_fusion.13
  12.9 1.9 bitcast_dynamic-update-slice_fusion.12
  14.7 1.9 bitcast_dynamic-update-slice_fusion.11
  16.6 1.9 bitcast_dynamic-update-slice_fusion.10
  18.5 1.9 bitcast_dynamic-update-slice_fusion.9
  20.3 1.9 bitcast_dynamic-update-slice_fusion.8
  22.2 2.0 bitcast_dynamic-update-slice_fusion.7
  24.2 1.9 bitcast_dynamic-update-slice_fusion.6
  26.1 1.9 bitcast_dynamic-update-slice_fusion.5
  27.9 1.9 bitcast_dynamic-update-slice_fusion.4
  29.8 1.9 bitcast_dynamic-update-slice_fusion.3
  31.7 1.9 bitcast_dynamic-update-slice_fusion.2
  33.5 1.9 bitcast_dynamic-update-slice_fusion.1
  35.4 1.9 bitcast_dynamic-update-slice_fusion
  37.3 7.3 %all-to-all-start = ((f32[16,512,256]{2,1,0:T(8,128)}), f32[16,512,256]{2,1,0:T(8,128)}, u32[]{:S(2)}, u32[]{:S(2)}) async-start(f32[16,512,256]{2,1,0:T(8,128)} %bitcast_dynamic-update-slice_fusion), calls=%async_computation | async-start | bytes 16777216 | tf_op jit(solution)/shard_map/all_to_all | solution.py:46
  44.6 0.0 all-reduce.4.cloned.1.call-start
  44.7 137.5 %all-to-all-done = f32[16,512,256]{2,1,0:T(8,128)} async-done(((f32[16,512,256]{2,1,0:T(8,128)}), f32[16,512,256]{2,1,0:T(8,128)}, u32[]{:S(2)}, u32[]{:S(2)}) %all-to-all-start) | async-done | bytes 8388640 | tf_op jit(solution)/shard_map/all_to_all | solution.py:46
  182.2 51.4 %all-gather.2.cloned.1.call-done = f32[3,256,8192]{2,1,0:T(8,128)} async-done(((f32[3,256,512]{2,1,0:T(8,128)}), f32[3,256,8192]{2,1,0:T(8,128)}) %all-gather.2.cloned.1.call-update) | async-done | bytes 25165840 | tf_op jit(solution)/shard_map/all_gather | solution.py:49
  233.6 0.0 copy-start.2
  233.6 14.9 %fusion.4 = f32[256,256]{1,0:T(8,128)} fusion(f32[8192,256]{1,0:T(8,128)} %bitcast.16, f32[3,256,8192]{2,1,0:T(8,128)} %all-gather.2.cloned.1.call-done, s32[8192]{0:T(1024)S(1)} %iota_add_fusion, s32[256]{0:T(256)S(1)} %iota_add_fusion.3), kind=kOutput, calls=%fused_computation.9 | convolution fusion | flops 6450839552 | bytes 17073152 | tf_op jit(solution)/shard_map/dot_general | solution.py:8
  248.5 0.0 all-reduce.4.cloned.1.call-update
  248.5 0.0 all-reduce.6.cloned.1.call-start
  248.6 72.2 %all-reduce.4.cloned.1.call-done = f32[256,256]{1,0:T(8,128)} async-done(((f32[256,256]{1,0:T(8,128)}), f32[256,256]{1,0:T(8,128)}) %all-reduce.4.cloned.1.call-update) | async-done | bytes 262160 | tf_op jit(solution)/shard_map/psum | solution.py:39
  320.8 0.0 copy-done.2
  320.8 1.5 fusion.50
  322.4 17.6 %convolution_subtract_fusion.2 = f32[8192,256]{1,0:T(8,128)S(1)} fusion(f32[8192,256]{1,0:T(8,128)} %bitcast.16, f32[256,256]{1,0:T(8,128)S(1)} %fusion.50, f32[3,256,8192]{2,1,0:T(8,128)} %all-gather.2.cloned.1.call-done, s32[8192]{0:T(1024)S(1)} %iota_add_fusion, s32[256]{0:T(256)S(1)} %iota_add_fusion.3), kind=kOutput, calls=%fused_computation.2 | convolution fusion | flops 6452936704 | bytes 25461760 | tf_op jit(solution)/shard_map/dot_general | solution.py:12
  340.0 0.0 copy-start
  340.0 3.4 copy-done
  343.4 12.3 %fusion.17 = f32[256,256]{1,0:T(8,128)} fusion(f32[8192,256]{1,0:T(8,128)S(1)} %convolution_subtract_fusion.2, f32[3,256,8192]{2,1,0:T(8,128)} %all-gather.2.cloned.1.call-done, s32[8192]{0:T(1024)S(1)} %iota_add_fusion, s32[256]{0:T(256)S(1)} %iota_add_fusion.2), kind=kOutput, calls=%fused_computation.21 | convolution fusion | flops 6450839552 | bytes 17073152 | tf_op jit(solution)/shard_map/dot_general | solution.py:8
  355.7 0.0 all-reduce.6.cloned.1.call-update
  355.8 0.2 all-reduce.8.cloned.1.call-start
  356.0 73.5 %all-reduce.6.cloned.1.call-done = f32[256,256]{1,0:T(8,128)} async-done(((f32[256,256]{1,0:T(8,128)}), f32[256,256]{1,0:T(8,128)}) %all-reduce.6.cloned.1.call-update) | async-done | bytes 262160 | tf_op jit(solution)/shard_map/psum | solution.py:39
  429.5 1.5 fusion.48
  431.0 17.2 %convolution_subtract_fusion.1 = f32[8192,256]{1,0:T(8,128)S(1)} fusion(f32[8192,256]{1,0:T(8,128)} %copy-done, f32[256,256]{1,0:T(8,128)S(1)} %fusion.48, f32[3,256,8192]{2,1,0:T(8,128)} %all-gather.2.cloned.1.call-done, s32[8192]{0:T(1024)S(1)} %iota_add_fusion, s32[256]{0:T(256)S(1)} %iota_add_fusion.2), kind=kOutput, calls=%fused_computation.1 | convolution fusion | flops 6452936704 | bytes 25461760 | tf_op jit(solution)/shard_map/dot_general | solution.py:12
  448.2 0.0 copy-start.1
  448.2 3.4 copy-done.1
  451.6 12.5 %fusion.20 = f32[256,256]{1,0:T(8,128)} fusion(f32[8192,256]{1,0:T(8,128)S(1)} %convolution_subtract_fusion.1, f32[3,256,8192]{2,1,0:T(8,128)} %all-gather.2.cloned.1.call-done, s32[8192]{0:T(1024)S(1)} %iota_add_fusion, s32[256]{0:T(256)S(1)} %iota_add_fusion.1), kind=kOutput, calls=%fused_computation.22 | convolution fusion | flops 6450839552 | bytes 17073152 | tf_op jit(solution)/shard_map/dot_general | solution.py:8
  464.1 0.0 all-reduce.8.cloned.1.call-update
  464.1 73.7 %all-reduce.8.cloned.1.call-done = f32[256,256]{1,0:T(8,128)} async-done(((f32[256,256]{1,0:T(8,128)}), f32[256,256]{1,0:T(8,128)}) %all-reduce.8.cloned.1.call-update) | async-done | bytes 262160 | tf_op jit(solution)/shard_map/psum | solution.py:39
  537.8 1.5 fusion.46
  539.4 19.2 %convolution_subtract_fusion = f32[8192,256]{1,0:T(8,128)} fusion(f32[8192,256]{1,0:T(8,128)} %copy-done.1, f32[256,256]{1,0:T(8,128)S(1)} %fusion.46, f32[3,256,8192]{2,1,0:T(8,128)} %all-gather.2.cloned.1.call-done, s32[8192]{0:T(1024)S(1)} %iota_add_fusion, s32[256]{0:T(256)S(1)} %iota_add_fusion.1), kind=kOutput, calls=%fused_computation | convolution fusion | flops 6452936704 | bytes 25461760 | tf_op jit(solution)/shard_map/dot_general | solution.py:12
  (4 shorter events, 0.0 us)
Async XLA Ops:
  6.5 227.1 %all-gather.2.cloned.1.call-start = ((), (), s32[]{:S(2)}) async-start(), calls=%async_computation.1 | async-start | bytes 26738688 | tf_op jit(solution)/shard_map/all_gather | solution.py:49
  37.3 144.9 %all-to-all-start = ((f32[16,512,256]{2,1,0:T(8,128)}), f32[16,512,256]{2,1,0:T(8,128)}, u32[]{:S(2)}, u32[]{:S(2)}) async-start(f32[16,512,256]{2,1,0:T(8,128)} %bitcast_dynamic-update-slice_fusion), calls=%async_computation | async-start | bytes 16777216 | tf_op jit(solution)/shard_map/all_to_all | solution.py:46
  44.6 276.2 %all-reduce.4.cloned.1.call-start = ((), (), s32[]{:S(2)}) async-start(), calls=%async_computation.2 | async-start | bytes 524288 | tf_op jit(solution)/shard_map/psum | solution.py:39
  233.6 87.2 %copy-start.2 = (f32[3,256,256]{2,1,0:T(8,128)S(1)}, f32[3,256,256]{2,1,0:T(8,128)}, u32[]{:S(2)}) copy-start(f32[3,256,256]{2,1,0:T(8,128)} %param.5) | copy-start | bytes 2359300
  248.5 180.9 %all-reduce.6.cloned.1.call-start = ((), (), s32[]{:S(2)}) async-start(), calls=%async_computation.3 | async-start | bytes 524288 | tf_op jit(solution)/shard_map/psum | solution.py:39
  340.0 3.4 copy-start
  355.8 182.1 %all-reduce.8.cloned.1.call-start = ((), (), s32[]{:S(2)}) async-start(), calls=%async_computation.4 | async-start | bytes 524288 | tf_op jit(solution)/shard_map/psum | solution.py:39
  448.2 3.4 copy-start.1
Sparse Core Ops, SparseCore 0:
  9.8 223.7 all-gather.1
  248.7 72.1 all-reduce.3
  355.9 73.5 all-reduce.5
  464.2 73.5 all-reduce.7
